TPU v7x, 128 devices: a whole 4x4x4 slice. The times are simulated.
128 devices in a mesh: seq: 8 (over y_hi, z), res: 16 (over y_lo, x, core).
Axes of the slice: x: 4, y: 4 (y_hi: 2, y_lo: 2; y = y_hi * 2 + y_lo), z: 4, core: 2. Of those that a mesh axis runs over, the one named last changes fastest.
Arguments:
- homology_table: bfloat16 [64, 2560, 256], P('seq', 'res'), may hold values from -6 to 6
- coupled_state: bfloat16 [2560, 2560, 128], P('seq', 'res'), may hold values from -6 to 6
- aligned_indicator: int32 [64, 2560], P('seq', 'res'), may hold values 0 or 1
- amino_indicator: int32 [2560], P('res'), may hold values 0 or 1
- horizontal_scaling_factor: float32 [256], replicated, may hold values from 0.25 to 1.75
- horizontal_projection_matrix: bfloat16 [256, 1024], replicated, may hold values from -6 to 6
- horizontal_sigmoid_shift: float32 [256], replicated, may hold values from -6 to 6
- horizontal_result_matrix: bfloat16 [256, 256], replicated, may hold values from -0.375 to 0.375
- horizontal_result_shift: float32 [256], replicated, may hold values from -3 to 3
- coupling_scaling_factor: float32 [128], replicated, may hold values from 0.25 to 1.75
- coupling_head_matrix: bfloat16 [128, 8], replicated, may hold values from -2 to 2
- downward_stretch_vector: float32 [256], replicated, may hold values from 0.25 to 1.75
- vertical_projection_matrix: bfloat16 [256, 1024], replicated, may hold values from -6 to 6
- vertical_sigmoid_shift: float32 [256], replicated, may hold values from -6 to 6
- vertical_result_matrix: bfloat16 [256, 256], replicated, may hold values from -0.375 to 0.375
- vertical_result_shift: float32 [256], replicated, may hold values from -3 to 3
- feedforward_scaling_factor: float32 [256], replicated, may hold values from 0.25 to 1.75
- feedforward_expand_matrix: bfloat16 [256, 1024], replicated, may hold values from -0.375 to 0.375
- feedforward_shrink_matrix: bfloat16 [1024, 256], replicated, may hold values from -0.1875 to 0.1875
Outputs:
- updated: bfloat16 [64, 2560, 256], P('seq', 'res')
All inputs are finite; a program needn't handle non-finite values. No bound on the sum of `aligned_indicator` or of `amino_indicator` on one device may be relied on, other than what follows from the above.
Results may differ from a plain program's by a relative error of at most 0.025.
Values may be sent and summed in bfloat16 or wider, within the bound.
No kernel may reach another device: no remote copies, remote signals or barrier semaphores. Data moves between devices by JAX's collectives and lax.ppermute only.
A program may use at most 256 MiB of HBM per device.

v0:
```python
import math

import jax
import jax.numpy as jnp
from jax import lax
from jax.sharding import PartitionSpec as P


def normalize_lanes(values, gain):
    values = values.astype(jnp.float32)
    center = values - jnp.mean(values, axis=-1, keepdims=True)
    spread = jnp.mean(center * center, axis=-1, keepdims=True)
    return center * lax.rsqrt(spread + 1e-05) * gain


def column_attend(query, pairs, mask_all, gate, heads):
    rows_q, resid, feature_dimension_size = query.shape
    rows_k = pairs.shape[0]
    head_size = feature_dimension_size // heads
    scale = 1.0 / math.sqrt(head_size)
    keys = pairs[..., :feature_dimension_size].reshape(rows_k, resid, heads, head_size)
    vals = pairs[..., feature_dimension_size:].reshape(rows_k, resid, heads, head_size)
    attention_logits = (
        jnp.einsum(
            "sihd,tihd->ihst",
            query.reshape(rows_q, resid, heads, head_size),
            keys,
            preferred_element_type=jnp.float32,
        )
        * scale
    )
    attention_logits = jnp.where(
        jnp.transpose(mask_all)[:, None, None, :] > 0, attention_logits, -1000000000.0
    )
    weights = jax.nn.softmax(attention_logits, axis=-1).astype(jnp.bfloat16)
    attended = jnp.einsum(
        "ihst,tihd->sihd", weights, vals, preferred_element_type=jnp.float32
    ).reshape(rows_q, resid, feature_dimension_size)
    return (attended * gate).astype(jnp.bfloat16)


def shards(
    homology_table,
    coupled_state,
    aligned_indicator,
    amino_indicator,
    horizontal_scaling_factor,
    horizontal_projection_matrix,
    horizontal_sigmoid_shift,
    horizontal_result_matrix,
    horizontal_result_shift,
    coupling_scaling_factor,
    coupling_head_matrix,
    downward_stretch_vector,
    vertical_projection_matrix,
    vertical_sigmoid_shift,
    vertical_result_matrix,
    vertical_result_shift,
    feedforward_scaling_factor,
    feedforward_expand_matrix,
    feedforward_shrink_matrix,
):
    homolog_lines, amino_lines, feature_dimension_size = homology_table.shape
    heads = coupling_head_matrix.shape[1]
    head_size = feature_dimension_size // heads
    scale = 1.0 / math.sqrt(head_size)
    pair_norm = normalize_lanes(coupled_state, coupling_scaling_factor).astype(jnp.bfloat16)
    tile_bias = jnp.einsum(
        "ijc,ch->hij", pair_norm, coupling_head_matrix, preferred_element_type=jnp.float32
    ).astype(jnp.bfloat16)
    bias_all_rows = lax.all_gather(tile_bias, "seq", axis=1, tiled=True)
    bias = lax.all_to_all(bias_all_rows, "res", split_axis=1, concat_axis=2, tiled=True).astype(
        jnp.float32
    )
    horizontal_standardized_state = normalize_lanes(
        homology_table, horizontal_scaling_factor
    ).astype(jnp.bfloat16)
    flat_in = horizontal_standardized_state.reshape(
        homolog_lines * amino_lines, feature_dimension_size
    )
    key_present_mask = (aligned_indicator * amino_indicator[None, :]).astype(jnp.bfloat16)
    query_proj = jnp.dot(
        flat_in,
        horizontal_projection_matrix[:, :feature_dimension_size],
        preferred_element_type=jnp.float32,
    )
    row_query = query_proj.astype(jnp.bfloat16).reshape(
        homolog_lines, amino_lines, feature_dimension_size
    )
    gate_proj = jnp.dot(
        flat_in,
        horizontal_projection_matrix[:, 3 * feature_dimension_size :],
        preferred_element_type=jnp.float32,
    )
    row_gate = jax.nn.sigmoid(gate_proj + horizontal_sigmoid_shift).reshape(
        homolog_lines, amino_lines, feature_dimension_size
    )
    pair_proj_local = jnp.dot(
        flat_in,
        horizontal_projection_matrix[:, feature_dimension_size : 3 * feature_dimension_size],
        preferred_element_type=jnp.float32,
    )
    local_pairs = pair_proj_local.astype(jnp.bfloat16).reshape(
        homolog_lines, amino_lines, 2 * feature_dimension_size
    )
    source_all, mask_all = (
        lax.all_gather(local_pairs, "res", axis=1, tiled=True),
        lax.all_gather(key_present_mask, "res", axis=1, tiled=True),
    )

    def one_row(items):
        query, source, mask_row = items
        total = source.shape[0]
        keys = source[:, :feature_dimension_size].reshape(total, heads, head_size)
        vals = source[:, feature_dimension_size:].reshape(total, heads, head_size)
        attention_logits = (
            jnp.einsum(
                "qhd,khd->hqk",
                query.reshape(amino_lines, heads, head_size),
                keys,
                preferred_element_type=jnp.float32,
            )
            * scale
            + bias
        )
        attention_logits = jnp.where(mask_row[None, None, :] > 0, attention_logits, -1000000000.0)
        weights = jax.nn.softmax(attention_logits, axis=-1).astype(jnp.bfloat16)
        return jnp.einsum(
            "hqk,khd->qhd", weights, vals, preferred_element_type=jnp.float32
        ).reshape(amino_lines, feature_dimension_size)

    row_o = lax.map(one_row, (row_query, source_all, mask_all))
    row_gated = (row_o * row_gate).astype(jnp.bfloat16)
    lateral_addend = (
        jnp.dot(
            row_gated.reshape(homolog_lines * amino_lines, feature_dimension_size),
            horizontal_result_matrix,
            preferred_element_type=jnp.float32,
        ).reshape(homolog_lines, amino_lines, feature_dimension_size)
        + horizontal_result_shift
    )
    homology_table_refreshed = (homology_table.astype(jnp.float32) + lateral_addend).astype(
        jnp.bfloat16
    )
    downward_source = normalize_lanes(homology_table_refreshed, downward_stretch_vector).astype(
        jnp.bfloat16
    )
    column_entry_mask = aligned_indicator.astype(jnp.bfloat16)
    proj_local = jnp.dot(
        downward_source.reshape(homolog_lines * amino_lines, feature_dimension_size),
        vertical_projection_matrix,
        preferred_element_type=jnp.float32,
    ).reshape(homolog_lines, amino_lines, 4 * feature_dimension_size)
    query = proj_local[..., :feature_dimension_size].astype(jnp.bfloat16)
    local_pairs = proj_local[..., feature_dimension_size : 3 * feature_dimension_size].astype(
        jnp.bfloat16
    )
    gate = jax.nn.sigmoid(proj_local[..., 3 * feature_dimension_size :] + vertical_sigmoid_shift)
    pairs_all, masks_all = (
        lax.all_gather(local_pairs, "seq", axis=0, tiled=True),
        lax.all_gather(column_entry_mask, "seq", axis=0, tiled=True),
    )
    col_gated = column_attend(query, pairs_all, masks_all, gate, heads)
    downward_change = (
        jnp.dot(
            col_gated.reshape(homolog_lines * amino_lines, feature_dimension_size),
            vertical_result_matrix,
            preferred_element_type=jnp.float32,
        ).reshape(homolog_lines, amino_lines, feature_dimension_size)
        + vertical_result_shift
    )
    post_downward_pass = (homology_table_refreshed.astype(jnp.float32) + downward_change).astype(
        jnp.bfloat16
    )
    trans_norm = normalize_lanes(post_downward_pass, feedforward_scaling_factor).astype(
        jnp.bfloat16
    )
    hidden = jax.nn.relu(
        jnp.dot(
            trans_norm.reshape(homolog_lines * amino_lines, feature_dimension_size),
            feedforward_expand_matrix,
            preferred_element_type=jnp.float32,
        )
    ).astype(jnp.bfloat16)
    trans_upd = jnp.dot(
        hidden, feedforward_shrink_matrix, preferred_element_type=jnp.float32
    ).reshape(homolog_lines, amino_lines, feature_dimension_size)
    return (post_downward_pass.astype(jnp.float32) + trans_upd).astype(jnp.bfloat16)


def solution(mesh):
    return jax.shard_map(
        shards,
        mesh=mesh,
        in_specs=(
            P("seq", "res", None),
            P("seq", "res", None),
            P("seq", "res"),
            P("res"),
            P(),
            P(),
            P(),
            P(),
            P(),
            P(),
            P(),
            P(),
            P(),
            P(),
            P(),
            P(),
            P(),
            P(),
            P(),
        ),
        out_specs=P("seq", "res", None),
        check_vma=False,
    )
```

profile of v0, /device:TPU:0, one launch (start us, length us, event | category | flops | bytes accessed | tf_op | source)
XLA Modules:
  0.0 1000.1 jit_solution(8079550182851768994)
XLA Ops:
  16.8 20.2 %fusion.6 = f32[320,160]{1,0:T(8,128)S(1)} fusion(bf16[320,160,128]{2,1,0:T(8,128)(2,1)S(1)} %copy-done.1, f32[320,160]{1,0:T(8,128)S(1)} %broadcast_multiply_fusion), kind=kLoop, calls=%fused_computation.15 | loop fusion | flops 26163200 | bytes 13516800 | tf_op jit(solution)/shard_map/reduce_sum | solution.py:12
  37.1 20.3 %fusion.32 = bf16[8,320,160]{2,0,1:T(8,128)(2,1)} fusion(bf16[320,160,128]{2,1,0:T(8,128)(2,1)S(1)} %copy-done.1, f32[128]{0:T(128)S(1)} %copy-done.20, f32[320,160]{1,0:T(8,128)S(1)} %add_rsqrt_fusion, f32[320,160]{1,0:T(8,128)S(1)} %broadcast_multiply_fusion, bf16[128,8]{0,1:T(8,128)(2,1)S(1)} %copy-done.16), kind=kOutput, calls=%fused_computation.57 | convolution fusion | flops 138035200 | bytes 14338560 | tf_op jit(solution)/shard_map/ijc,ch->hij/dot_general | solution.py:68
  61.3 125.0 %all-gather.7.cloned.1.call-done = bf16[8,2560,160]{2,0,1:T(8,128)(2,1)} async-done(((bf16[8,320,160]{2,0,1:T(8,128)(2,1)}), bf16[8,2560,160]{2,0,1:T(8,128)(2,1)}) %all-gather.7.cloned.1.call-update) | async-done | bytes 6553616 | tf_op jit(solution)/shard_map/all_gather | solution.py:71
  191.8 211.2 %all-gather = bf16[16,160,8]{1,2,0:T(8,128)(2,1)S(1)} all-gather(bf16[1,160,8]{1,2,0:T(8,128)(2,1)S(1)} %get-tuple-element.79), channel_id=1, replica_groups=mesh['seq'=8,'res'=16] {'res'}, dimensions={0}, use_global_device_ids=true | all-gather | bytes 43520 | tf_op jit(solution)/shard_map/all_gather | solution.py:108
  406.7 13.3 %convert_bitcast_fusion = f32[8,160,16,160]{3,0,1,2:T(8,128)} fusion(bf16[8,16,160,160]{3,0,2,1:T(8,128)(2,1)} %bitcast.30), kind=kLoop, calls=%fused_computation.18 | loop fusion | flops 3276800 | bytes 19660800 | tf_op jit(solution)/shard_map/convert_element_type | solution.py:72
  420.0 21.4 %copy.63 = f32[8,160,16,160]{3,2,1,0:T(8,128)} copy(f32[8,160,16,160]{3,0,1,2:T(8,128)} %convert_bitcast_fusion) | data formatting | bytes 26214400 | tf_op jit(solution)/shard_map/convert_element_type | solution.py:72
  441.4 22.5 %reshape.141 = f32[8,160,2560]{2,1,0:T(8,128)} reshape(f32[8,160,16,160]{3,2,1,0:T(8,128)} %copy.63) | data formatting | bytes 26214400 | tf_op jit(solution)/shard_map/convert_element_type | solution.py:72
  463.9 27.8 %copy.64 = bf16[8,2560,512]{1,2,0:T(8,128)(2,1)} copy(bf16[8,2560,512]{2,0,1:T(8,128)(2,1)} %all-gather.5.cloned.1.call-done) | data formatting | bytes 41943040 | tf_op jit(solution)/shard_map/while | solution.py:132
  491.7 305.6 %while.10 = (s32[]{:T(128)}, f32[8,160,256]{1,2,0:T(8,128)}, bf16[8,2560,512]{1,2,0:T(8,128)(2,1)}, bf16[8,2560]{1,0:T(8,128)(2,1)S(1)}, bf16[8,160,256]{2,1,0:T...) while((s32[]{:T(128)}, f32[8,160,256]{1,2,0:T(8,128)}, bf16[8,2560,512]{1,2,0:T(8,128)(2,1)}, ...), condition=%wide.region_7.8_spmd, body=%wide.region_4.7_spmd.sunk | while | flops 445658880 | bytes 66556504 | solution.py:132
  494.9 11.5 %add_select_fusion.2 = f32[8,160,2560]{2,1,0:T(8,128)} fusion(f32[8,160,2560]{2,1,0:T(8,128)} %get-tuple-element.148, bf16[160,8,32]{0,2,1:T(8,128)(2,1)S(1)} %bitcast.98, bf16[2560,8,32]{0,2,1:T(8,128)(2,1)S(1)} %bitcast.95, pred[2560]{0:T(1024)(128)(4,1)S(1)} %compare_reduce_fusion.2), kind=kOutput, calls=%fused_computation.3.clone.1 | convolution fusion | flops 219545600 | bytes 27609600 | tf_op jit(solution)/shard_map/while/body/eval_jaxpr/qhd,khd->hqk/dot_general | solution.py:117
  506.4 10.8 %fusion.112 = f32[8,160]{1,0:T(8,128)S(1)} fusion(f32[8,160,2560]{2,1,0:T(8,128)} %add_select_fusion.2), kind=kOutput, calls=%fused_computation.105.clone.1 | output fusion | flops 6556159 | bytes 13112320 | tf_op jit(solution)/shard_map/while/body/eval_jaxpr/sub | solution.py:127
  517.2 12.0 %fusion.113 = f32[8,32,160]{2,1,0:T(8,128)S(1)} fusion(bf16[2560,8,32]{0,2,1:T(8,128)(2,1)S(1)} %bitcast.97, f32[8,160]{1,0:T(8,128)S(1)} %fusion.112, f32[8,160,2560]{2,1,0:T(8,128)} %add_select_fusion.2), kind=kOutput, calls=%fused_computation.4.clone.1 | convolution fusion | flops 219549440 | bytes 14586880 | tf_op jit(solution)/shard_map/while/body/eval_jaxpr/hqk,khd->qhd/dot_general | solution.py:128
  533.1 11.5 %add_select_fusion.2 = f32[8,160,2560]{2,1,0:T(8,128)} fusion(f32[8,160,2560]{2,1,0:T(8,128)} %get-tuple-element.148, bf16[160,8,32]{0,2,1:T(8,128)(2,1)S(1)} %bitcast.98, bf16[2560,8,32]{0,2,1:T(8,128)(2,1)S(1)} %bitcast.95, pred[2560]{0:T(1024)(128)(4,1)S(1)} %compare_reduce_fusion.2), kind=kOutput, calls=%fused_computation.3.clone.1 | convolution fusion | flops 219545600 | bytes 27609600 | tf_op jit(solution)/shard_map/while/body/eval_jaxpr/qhd,khd->hqk/dot_general | solution.py:117
  544.6 10.8 %fusion.112 = f32[8,160]{1,0:T(8,128)S(1)} fusion(f32[8,160,2560]{2,1,0:T(8,128)} %add_select_fusion.2), kind=kOutput, calls=%fused_computation.105.clone.1 | output fusion | flops 6556159 | bytes 13112320 | tf_op jit(solution)/shard_map/while/body/eval_jaxpr/sub | solution.py:127
  555.4 12.0 %fusion.113 = f32[8,32,160]{2,1,0:T(8,128)S(1)} fusion(bf16[2560,8,32]{0,2,1:T(8,128)(2,1)S(1)} %bitcast.97, f32[8,160]{1,0:T(8,128)S(1)} %fusion.112, f32[8,160,2560]{2,1,0:T(8,128)} %add_select_fusion.2), kind=kOutput, calls=%fused_computation.4.clone.1 | convolution fusion | flops 219549440 | bytes 14586880 | tf_op jit(solution)/shard_map/while/body/eval_jaxpr/hqk,khd->qhd/dot_general | solution.py:128
  571.3 11.5 %add_select_fusion.2 = f32[8,160,2560]{2,1,0:T(8,128)} fusion(f32[8,160,2560]{2,1,0:T(8,128)} %get-tuple-element.148, bf16[160,8,32]{0,2,1:T(8,128)(2,1)S(1)} %bitcast.98, bf16[2560,8,32]{0,2,1:T(8,128)(2,1)S(1)} %bitcast.95, pred[2560]{0:T(1024)(128)(4,1)S(1)} %compare_reduce_fusion.2), kind=kOutput, calls=%fused_computation.3.clone.1 | convolution fusion | flops 219545600 | bytes 27609600 | tf_op jit(solution)/shard_map/while/body/eval_jaxpr/qhd,khd->hqk/dot_general | solution.py:117
  582.8 10.8 %fusion.112 = f32[8,160]{1,0:T(8,128)S(1)} fusion(f32[8,160,2560]{2,1,0:T(8,128)} %add_select_fusion.2), kind=kOutput, calls=%fused_computation.105.clone.1 | output fusion | flops 6556159 | bytes 13112320 | tf_op jit(solution)/shard_map/while/body/eval_jaxpr/sub | solution.py:127
  593.6 12.0 %fusion.113 = f32[8,32,160]{2,1,0:T(8,128)S(1)} fusion(bf16[2560,8,32]{0,2,1:T(8,128)(2,1)S(1)} %bitcast.97, f32[8,160]{1,0:T(8,128)S(1)} %fusion.112, f32[8,160,2560]{2,1,0:T(8,128)} %add_select_fusion.2), kind=kOutput, calls=%fused_computation.4.clone.1 | convolution fusion | flops 219549440 | bytes 14586880 | tf_op jit(solution)/shard_map/while/body/eval_jaxpr/hqk,khd->qhd/dot_general | solution.py:128
  609.5 11.5 %add_select_fusion.2 = f32[8,160,2560]{2,1,0:T(8,128)} fusion(f32[8,160,2560]{2,1,0:T(8,128)} %get-tuple-element.148, bf16[160,8,32]{0,2,1:T(8,128)(2,1)S(1)} %bitcast.98, bf16[2560,8,32]{0,2,1:T(8,128)(2,1)S(1)} %bitcast.95, pred[2560]{0:T(1024)(128)(4,1)S(1)} %compare_reduce_fusion.2), kind=kOutput, calls=%fused_computation.3.clone.1 | convolution fusion | flops 219545600 | bytes 27609600 | tf_op jit(solution)/shard_map/while/body/eval_jaxpr/qhd,khd->hqk/dot_general | solution.py:117
  631.8 12.0 %fusion.113 = f32[8,32,160]{2,1,0:T(8,128)S(1)} fusion(bf16[2560,8,32]{0,2,1:T(8,128)(2,1)S(1)} %bitcast.97, f32[8,160]{1,0:T(8,128)S(1)} %fusion.112, f32[8,160,2560]{2,1,0:T(8,128)} %add_select_fusion.2), kind=kOutput, calls=%fused_computation.4.clone.1 | convolution fusion | flops 219549440 | bytes 14586880 | tf_op jit(solution)/shard_map/while/body/eval_jaxpr/hqk,khd->qhd/dot_general | solution.py:128
  647.7 11.5 %add_select_fusion.2 = f32[8,160,2560]{2,1,0:T(8,128)} fusion(f32[8,160,2560]{2,1,0:T(8,128)} %get-tuple-element.148, bf16[160,8,32]{0,2,1:T(8,128)(2,1)S(1)} %bitcast.98, bf16[2560,8,32]{0,2,1:T(8,128)(2,1)S(1)} %bitcast.95, pred[2560]{0:T(1024)(128)(4,1)S(1)} %compare_reduce_fusion.2), kind=kOutput, calls=%fused_computation.3.clone.1 | convolution fusion | flops 219545600 | bytes 27609600 | tf_op jit(solution)/shard_map/while/body/eval_jaxpr/qhd,khd->hqk/dot_general | solution.py:117
  670.0 12.0 %fusion.113 = f32[8,32,160]{2,1,0:T(8,128)S(1)} fusion(bf16[2560,8,32]{0,2,1:T(8,128)(2,1)S(1)} %bitcast.97, f32[8,160]{1,0:T(8,128)S(1)} %fusion.112, f32[8,160,2560]{2,1,0:T(8,128)} %add_select_fusion.2), kind=kOutput, calls=%fused_computation.4.clone.1 | convolution fusion | flops 219549440 | bytes 14586880 | tf_op jit(solution)/shard_map/while/body/eval_jaxpr/hqk,khd->qhd/dot_general | solution.py:128
  685.9 11.5 %add_select_fusion.2 = f32[8,160,2560]{2,1,0:T(8,128)} fusion(f32[8,160,2560]{2,1,0:T(8,128)} %get-tuple-element.148, bf16[160,8,32]{0,2,1:T(8,128)(2,1)S(1)} %bitcast.98, bf16[2560,8,32]{0,2,1:T(8,128)(2,1)S(1)} %bitcast.95, pred[2560]{0:T(1024)(128)(4,1)S(1)} %compare_reduce_fusion.2), kind=kOutput, calls=%fused_computation.3.clone.1 | convolution fusion | flops 219545600 | bytes 27609600 | tf_op jit(solution)/shard_map/while/body/eval_jaxpr/qhd,khd->hqk/dot_general | solution.py:117
  708.2 12.0 %fusion.113 = f32[8,32,160]{2,1,0:T(8,128)S(1)} fusion(bf16[2560,8,32]{0,2,1:T(8,128)(2,1)S(1)} %bitcast.97, f32[8,160]{1,0:T(8,128)S(1)} %fusion.112, f32[8,160,2560]{2,1,0:T(8,128)} %add_select_fusion.2), kind=kOutput, calls=%fused_computation.4.clone.1 | convolution fusion | flops 219549440 | bytes 14586880 | tf_op jit(solution)/shard_map/while/body/eval_jaxpr/hqk,khd->qhd/dot_general | solution.py:128
  724.1 11.5 %add_select_fusion.2 = f32[8,160,2560]{2,1,0:T(8,128)} fusion(f32[8,160,2560]{2,1,0:T(8,128)} %get-tuple-element.148, bf16[160,8,32]{0,2,1:T(8,128)(2,1)S(1)} %bitcast.98, bf16[2560,8,32]{0,2,1:T(8,128)(2,1)S(1)} %bitcast.95, pred[2560]{0:T(1024)(128)(4,1)S(1)} %compare_reduce_fusion.2), kind=kOutput, calls=%fused_computation.3.clone.1 | convolution fusion | flops 219545600 | bytes 27609600 | tf_op jit(solution)/shard_map/while/body/eval_jaxpr/qhd,khd->hqk/dot_general | solution.py:117
  746.4 12.0 %fusion.113 = f32[8,32,160]{2,1,0:T(8,128)S(1)} fusion(bf16[2560,8,32]{0,2,1:T(8,128)(2,1)S(1)} %bitcast.97, f32[8,160]{1,0:T(8,128)S(1)} %fusion.112, f32[8,160,2560]{2,1,0:T(8,128)} %add_select_fusion.2), kind=kOutput, calls=%fused_computation.4.clone.1 | convolution fusion | flops 219549440 | bytes 14586880 | tf_op jit(solution)/shard_map/while/body/eval_jaxpr/hqk,khd->qhd/dot_general | solution.py:128
  762.3 11.5 %add_select_fusion.2 = f32[8,160,2560]{2,1,0:T(8,128)} fusion(f32[8,160,2560]{2,1,0:T(8,128)} %get-tuple-element.148, bf16[160,8,32]{0,2,1:T(8,128)(2,1)S(1)} %bitcast.98, bf16[2560,8,32]{0,2,1:T(8,128)(2,1)S(1)} %bitcast.95, pred[2560]{0:T(1024)(128)(4,1)S(1)} %compare_reduce_fusion.2), kind=kOutput, calls=%fused_computation.3.clone.1 | convolution fusion | flops 219545600 | bytes 27609600 | tf_op jit(solution)/shard_map/while/body/eval_jaxpr/qhd,khd->hqk/dot_general | solution.py:117
  784.6 12.0 %fusion.113 = f32[8,32,160]{2,1,0:T(8,128)S(1)} fusion(bf16[2560,8,32]{0,2,1:T(8,128)(2,1)S(1)} %bitcast.97, f32[8,160]{1,0:T(8,128)S(1)} %fusion.112, f32[8,160,2560]{2,1,0:T(8,128)} %add_select_fusion.2), kind=kOutput, calls=%fused_computation.4.clone.1 | convolution fusion | flops 219549440 | bytes 14586880 | tf_op jit(solution)/shard_map/while/body/eval_jaxpr/hqk,khd->qhd/dot_general | solution.py:128
  805.6 34.1 %all_gather.19 = bf16[64,160]{1,0:T(8,128)(2,1)S(1)} all-gather(bf16[8,160]{1,0:T(8,128)(2,1)S(1)} %copy-done.8), channel_id=1, replica_groups=mesh['seq'=8,'res'=16] {'seq'}, dimensions={0}, use_global_device_ids=true | all-gather | bytes 23040 | tf_op jit(solution)/shard_map/all_gather | solution.py:161
  846.3 83.6 %all-gather.9.cloned.1.call-done = bf16[64,160,512]{2,1,0:T(8,128)(2,1)} async-done(((bf16[8,160,512]{2,1,0:T(8,128)(2,1)}), bf16[64,160,512]{2,1,0:T(8,128)(2,1)}) %all-gather.9.cloned.1.call-update) | async-done | bytes 10485776 | tf_op jit(solution)/shard_map/all_gather | solution.py:160
  938.6 11.3 %copy.82 = bf16[64,160,256]{0,2,1:T(8,128)(2,1)} copy(bf16[64,160,256]{2,1,0:T(8,128)(2,1)} %get-tuple-element.76) | data formatting | bytes 10485760 | tf_op jit(solution)/shard_map/reshape | solution.py:21
  949.9 11.3 %copy.81 = bf16[64,160,256]{0,2,1:T(8,128)(2,1)} copy(bf16[64,160,256]{2,1,0:T(8,128)(2,1)} %get-tuple-element.77) | data formatting | bytes 10485760 | tf_op jit(solution)/shard_map/reshape | solution.py:22
  (144 shorter events, 164.0 us)
Async XLA Ops:
  6.5 794.6 %copy-start = (bf16[256,1024]{1,0:T(8,128)(2,1)S(1)}, bf16[256,1024]{1,0:T(8,128)(2,1)}, u32[]{:S(2)}) copy-start(bf16[256,1024]{1,0:T(8,128)(2,1)} %param.33) | copy-start | bytes 1572868
  6.5 179.8 %all-gather.7.cloned.1.call-start = ((), (), s32[]{:S(2)}) async-start(), calls=%async_computation.2 | async-start | bytes 11796480 | tf_op jit(solution)/shard_map/all_gather | solution.py:71
  6.5 10.2 %copy-start.1 = (bf16[320,160,128]{2,1,0:T(8,128)(2,1)S(1)}, bf16[320,160,128]{2,1,0:T(8,128)(2,1)}, u32[]{:S(2)}) copy-start(bf16[320,160,128]{2,1,0:T(8,128)(2,1)} %param.22) | copy-start | bytes 39321604
  16.8 20.3 %copy-start.16 = (bf16[128,8]{0,1:T(8,128)(2,1)S(1)}, bf16[128,8]{0,1:T(8,128)(2,1)}, u32[]{:S(2)}) copy-start(bf16[128,8]{0,1:T(8,128)(2,1)} %param.31) | copy-start | bytes 6148
  16.8 20.3 %copy-start.20 = (f32[128]{0:T(128)S(1)}, f32[128]{0:T(128)}, u32[]{:S(2)}) copy-start(f32[128]{0:T(128)} %param.30) | copy-start | bytes 1540
  37.1 20.4 %copy-start.2 = (bf16[8,160,256]{2,1,0:T(8,128)(2,1)S(1)}, bf16[8,160,256]{2,1,0:T(8,128)(2,1)}, u32[]{:S(2)}) copy-start(bf16[8,160,256]{2,1,0:T(8,128)(2,1)} %param.21) | copy-start | bytes 1966084
  57.4 1.0 copy-start.10
  57.4 1.5 copy-start.5
  57.5 406.4 %all-gather.5.cloned.1.call-start = ((), (), s32[]{:S(2)}) async-start(), calls=%async_computation.1 | async-start | bytes 22282240 | tf_op jit(solution)/shard_map/all_gather | solution.py:107
  61.3 129.9 %copy-start.9 = (s32[8,160]{1,0:T(8,128)S(1)}, s32[8,160]{1,0:T(8,128)}, u32[]{:S(2)}) copy-start(s32[8,160]{1,0:T(8,128)} %param.23) | copy-start | bytes 15364
  61.3 129.9 %copy-start.14 = (s32[160]{0:T(256)S(1)}, s32[160]{0:T(256)}, u32[]{:S(2)}) copy-start(s32[160]{0:T(256)} %param.24) | copy-start | bytes 1924
  61.3 341.9 %copy-start.6 = (bf16[256,1024]{1,0:T(8,128)(2,1)S(1)}, bf16[256,1024]{1,0:T(8,128)(2,1)}, u32[]{:S(2)}) copy-start(bf16[256,1024]{1,0:T(8,128)(2,1)} %param.26) | copy-start | bytes 1572868
  61.3 341.9 %copy-start.17 = (f32[256]{0:T(256)S(1)}, f32[256]{0:T(256)}, u32[]{:S(2)}) copy-start(f32[256]{0:T(256)} %param.27) | copy-start | bytes 3076
  186.3 220.4 %all-to-all-start = ((bf16[8,2560,160]{2,0,1:T(8,128)(2,1)}), bf16[8,2560,160]{2,0,1:T(8,128)(2,1)}, u32[]{:S(2)}, u32[]{:S(2)}) async-start(bf16[8,2560,160]{2,0,1:T(8,128)(2,1)} %all-gather.7.cloned.1.call-done), calls=%async_computation | async-start | bytes 20971520 | tf_op jit(solution)/shard_map/all_to_all | solution.py:72
  191.2 738.7 %all-gather.9.cloned.1.call-start = ((), (), s32[]{:S(2)}) async-start(), calls=%async_computation.3 | async-start | bytes 11796480 | tf_op jit(solution)/shard_map/all_gather | solution.py:160
  491.7 305.6 %copy-start.7 = (bf16[256,256]{1,0:T(8,128)(2,1)S(1)}, bf16[256,256]{1,0:T(8,128)(2,1)}, u32[]{:S(2)}) copy-start(bf16[256,256]{1,0:T(8,128)(2,1)} %param.28) | copy-start | bytes 393220
  491.7 305.6 %copy-start.11 = (f32[256]{0:T(256)S(1)}, f32[256]{0:T(256)}, u32[]{:S(2)}) copy-start(f32[256]{0:T(256)} %param.29) | copy-start | bytes 3076
  797.3 3.8 copy-start.12
  800.5 3.9 copy-start.3
  804.3 1.2 copy-start.8
  984.7 1.7 copy-start.4
  984.7 1.7 copy-start.15
  984.7 1.7 copy-start.18
  984.7 1.7 copy-start.19
  986.4 3.0 copy-start.13
Sparse Core Ops, SparseCore 0:
  57.6 128.6 all-gather.6
  188.0 224.8 all-gather.4
  805.7 124.0 all-gather.8
where the time goes:
time: 1000 us
  blocking collectives  245 us (24%)
  matrix products  241 us (24%)
  waiting for transfers between devices  209 us (21%)
  local copies, waits for them, and re-layouts  152 us (15%)
  other arithmetic  135 us (14%)
  between operations  13.5 us (1%)
    all_gather x1, blocking collectives, shards(): lax.all_gather(key_present_mask, 'res', axis=1, tiled=True)  211 us
    all_gather x1, waiting for transfers between devices, shards(): bias_all_rows = lax.all_gather(tile_bias, 'seq', axis=1, tiled=True)  125 us
    dot_general x8, matrix products, one_row(): jnp.einsum('hqk,khd->qhd', weights, vals, preferred_element_type=jnp.floa...  96.1 us
    dot_general x8, matrix products, one_row(): jnp.einsum('qhd,khd->hqk', query.reshape(amino_lines, heads, head_size),...  91.8 us
    sub x8, other arithmetic, one_row(): weights = jax.nn.softmax(attention_logits, axis=-1).astype(jnp.bfloat16)  86.5 us
    all_gather x1, waiting for transfers between devices, shards(): lax.all_gather(local_pairs, 'seq', axis=0, tiled=True)  83.6 us
    convert_element_type x2, local copies, waits for them, and re-layouts, shards(): lax.all_to_all(bias_all_rows, 'res', split_axis=1, concat_axis=2, tiled=T...  43.9 us
    all_gather x1, blocking collectives, shards(): lax.all_gather(column_entry_mask, 'seq', axis=0, tiled=True)  34.1 us
  transfers between devices with their start and end apart: 4, of which 2 were waited for; matrix products, arithmetic and copies ran while one was open for 7% of the time, Pallas kernels for 0%

commit v1 on v0

v1 whole, which is shorter than its diff:
```python
import functools
import math

import jax
import jax.numpy as jnp
from jax import lax
from jax.experimental import pallas as pl
from jax.experimental.pallas import tpu as pltpu
from jax.sharding import PartitionSpec as P

F32 = jnp.float32
BF16 = jnp.bfloat16
EPS = 1e-05
LOG2E = 1.4426950408889634
LANES = 128
MASK_LANE = 96
ONE_LANE = 97
MASKED = -1e30
VMEM = 56 * 2**20


def dot(a, b):
    return jnp.dot(a, b, preferred_element_type=F32)


def dot_nt(a, b):
    return lax.dot_general(a, b, (((1,), (1,)), ((), ())), preferred_element_type=F32)


def dot_tn(a, b):
    return lax.dot_general(a, b, (((0,), (0,)), ((), ())), preferred_element_type=F32)


def normalize(values, gain):
    center = values - jnp.mean(values, axis=-1, keepdims=True)
    spread = jnp.mean(center * center, axis=-1, keepdims=True)
    return center * lax.rsqrt(spread + EPS) * gain


def lanes_of(shape):
    return lax.broadcasted_iota(jnp.int32, shape, len(shape) - 1)


def pair_kernel(pair_ref, project_ref, bias_ref, rows_ref, *, channels, heads):
    for i in range(pair_ref.shape[0]):
        both = dot_nt(project_ref[...], pair_ref[i])
        center = both[:channels]
        spread = jnp.sum(center * center, axis=0, keepdims=True) * (1.0 / channels)
        raw = both[channels : channels + heads] + both[channels + heads :]
        rows_ref[:, i, :] = raw * lax.rsqrt(spread + EPS)
    bias_ref[...] = rows_ref[...].astype(BF16)


def pair_bias(coupled, gain, head_matrix, step):
    rows, cols, channels = coupled.shape
    heads = head_matrix.shape[1]
    gained = gain[:, None] * head_matrix.astype(F32) * LOG2E
    gained = (gained - jnp.mean(gained, axis=0, keepdims=True)).T
    high = gained.astype(BF16)
    low = (gained - high.astype(F32)).astype(BF16)
    centering = (jnp.eye(channels, dtype=F32) - 1.0 / channels).astype(BF16)
    project = jnp.concatenate([centering, high, low], axis=0)
    return pl.pallas_call(
        functools.partial(pair_kernel, channels=channels, heads=heads),
        grid=(rows // step,),
        in_specs=[
            pl.BlockSpec((step, cols, channels), lambda i: (i, 0, 0)),
            pl.BlockSpec(project.shape, lambda i: (0, 0)),
        ],
        out_specs=pl.BlockSpec((heads, step, cols), lambda i: (0, i, 0)),
        out_shape=jax.ShapeDtypeStruct((heads, rows, cols), BF16),
        scratch_shapes=[pltpu.VMEM((heads, step, cols), F32)],
        compiler_params=pltpu.CompilerParams(vmem_limit_bytes=VMEM),
        name="pair_bias",
    )(coupled, project)


def pack_kernel(table_ref, mask_ref, gain_ref, weight_ref, packed_ref, *, heads, scale):
    head_size = table_ref.shape[-1] // heads
    normed = normalize(table_ref[0].astype(F32), gain_ref[...]).astype(BF16)
    flat = dot(normed, weight_ref[...])
    lane = lanes_of((flat.shape[0], LANES))
    factor = jnp.where(lane < head_size, scale, 1.0)
    extra = jnp.where(
        lane == MASK_LANE, mask_ref[0], jnp.where(lane == ONE_LANE, 1.0, 0.0)
    )
    for h in range(heads):
        packed_ref[h, 0] = (flat[:, h * LANES : (h + 1) * LANES] * factor + extra).astype(BF16)


def pack_heads(table, mask, gain, weight, heads, scale):
    lines, residues, channels = table.shape
    head_size = channels // heads
    parts = weight.reshape(channels, 4, heads, head_size)
    parts = jnp.transpose(parts, (0, 2, 1, 3))
    parts = jnp.where(jnp.arange(4)[None, None, :, None] < 3, parts, 0)
    parts = parts.reshape(channels, heads * 4 * head_size)
    return pl.pallas_call(
        functools.partial(pack_kernel, heads=heads, scale=scale),
        grid=(lines,),
        in_specs=[
            pl.BlockSpec((1, residues, channels), lambda s: (s, 0, 0)),
            pl.BlockSpec((1, residues, 1), lambda s: (s, 0, 0)),
            pl.BlockSpec((1, channels), lambda s: (0, 0)),
            pl.BlockSpec(parts.shape, lambda s: (0, 0)),
        ],
        out_specs=pl.BlockSpec((heads, 1, residues, LANES), lambda s: (0, s, 0, 0)),
        out_shape=jax.ShapeDtypeStruct((heads, lines, residues, LANES), BF16),
        compiler_params=pltpu.CompilerParams(vmem_limit_bytes=VMEM),
        name="pack_heads",
    )(table, mask[:, :, None], gain[None, :], parts)


def row_kernel(own_ref, other_ref, bias_ref, out_ref, bias32_ref, score_ref, weight_ref, *, per, head_size, tile, chunk):
    blocks, lines, residues, _ = own_ref.shape
    queries = per * residues
    half = blocks * residues
    pieces = out_ref.shape[0]
    span = residues // pieces
    group = LANES // head_size
    for b in range(per):
        bias32_ref[b * residues : (b + 1) * residues] = bias_ref[b].astype(F32)
    lane = lanes_of((queries, LANES))
    first = pl.program_id(0) * per
    for pack in range(lines // group):
        total = jnp.zeros((queries, LANES), F32)
        for member in range(group):
            s = pack * group + member
            raw = jnp.concatenate([own_ref[first + b, s] for b in range(per)], axis=0)
            moved = pltpu.roll(raw.astype(F32), head_size, 1)
            query = jnp.where(
                (lane >= head_size) & (lane < 2 * head_size),
                moved,
                jnp.where(lane == MASK_LANE, 1.0, 0.0),
            ).astype(BF16)
            sources = [r[:, s].reshape(half, LANES) for r in (own_ref, other_ref)]
            for k in range(0, 2 * half, chunk):
                keys = sources[k // half][k % half : k % half + chunk]
                score_ref[:, k : k + chunk] = dot_nt(query, keys) + bias32_ref[:, k : k + chunk]
            for q in range(0, queries, tile):
                scores = score_ref[q : q + tile, :]
                top = jnp.max(scores, axis=1, keepdims=True)
                weight_ref[q : q + tile, :] = jnp.exp2(scores - top).astype(BF16)
            mixed = dot(weight_ref[:, :half], sources[0]) + dot(weight_ref[:, half:], sources[1])
            mixed = mixed / mixed[:, ONE_LANE : ONE_LANE + 1]
            mixed = pltpu.roll(mixed, (member * head_size - 2 * head_size) % LANES, 1)
            here = (lane >= member * head_size) & (lane < (member + 1) * head_size)
            total = jnp.where(here, mixed, total)
        for b in range(per):
            for piece in range(pieces):
                start = b * residues + piece * span
                out_ref[piece, b, pack * span : (pack + 1) * span, :] = total[start : start + span].astype(BF16)


def row_attention(own, other, bias, pieces, head_size, per):
    blocks, lines, residues, _ = own.shape
    queries = per * residues
    keys = 2 * blocks * residues
    rows = lines * head_size // LANES * residues // pieces
    whole = pl.BlockSpec(own.shape, lambda i: (0, 0, 0, 0))
    return pl.pallas_call(
        functools.partial(row_kernel, per=per, head_size=head_size, tile=16, chunk=256),
        grid=(blocks // per,),
        in_specs=[
            whole,
            whole,
            pl.BlockSpec((per, residues, keys), lambda i: (i, 0, 0)),
        ],
        out_specs=pl.BlockSpec((pieces, per, rows, LANES), lambda i: (0, i, 0, 0)),
        out_shape=jax.ShapeDtypeStruct((pieces, blocks, rows, LANES), BF16),
        scratch_shapes=[
            pltpu.VMEM((queries, keys), F32),
            pltpu.VMEM((queries, keys), F32),
            pltpu.VMEM((queries, keys), BF16),
        ],
        compiler_params=pltpu.CompilerParams(vmem_limit_bytes=VMEM),
        name="row_attention",
    )(own, other, bias)


def column_kernel(
    mixed_ref, table_ref, mask_ref,
    row_gain_ref, row_gate_ref, row_shift_ref, row_out_ref, row_bias_ref,
    col_gain_ref, col_weight_ref, col_shift_ref, col_out_ref, col_bias_ref,
    ff_gain_ref, expand_ref, shrink_ref, out_ref, *, heads, scale,
):
    groups, span, lines, channels = table_ref.shape
    rows = groups * lines
    head_size = channels // heads
    table = table_ref[...].astype(F32)
    table = jnp.concatenate([table[:, i].reshape(rows, channels) for i in range(span)], axis=0)
    mixed = mixed_ref[...].reshape(span * rows, channels).astype(F32)

    row_in = normalize(table, row_gain_ref[...]).astype(BF16)
    gate = jax.nn.sigmoid(dot(row_in, row_gate_ref[...]) + row_shift_ref[...])
    gated = (mixed * gate).astype(BF16)
    after_rows = table + (dot(gated, row_out_ref[...]) + row_bias_ref[...])
    after_rows = after_rows.astype(BF16).astype(F32)

    col_in = normalize(after_rows, col_gain_ref[...]).astype(BF16)
    projected = dot(col_in, col_weight_ref[...])
    query = (projected[:, :channels] * scale).astype(BF16)
    key = projected[:, channels : 2 * channels].astype(BF16)
    value = projected[:, 2 * channels : 3 * channels].astype(BF16)
    gate = jax.nn.sigmoid(projected[:, 3 * channels :] + col_shift_ref[...])

    shape = (heads * rows, channels)
    row_head = lax.broadcasted_iota(jnp.int32, shape, 0) // rows
    same = row_head == lax.broadcasted_iota(jnp.int32, shape, 1) // head_size
    same = jnp.where(same, 1.0, 0.0).astype(BF16)
    masks = mask_ref[:, 0].astype(F32).reshape(rows, channels)
    mask_lane = lanes_of((rows, channels))
    attended = []
    for i in range(span):
        here = slice(i * rows, (i + 1) * rows)
        spread_key = jnp.concatenate([key[here]] * heads, axis=0) * same
        spread_value = jnp.concatenate([value[here]] * heads, axis=0) * same
        scores = dot_nt(spread_key, query[here]).reshape(heads, rows, rows)
        place = pl.program_id(0) * span + i
        present = jnp.sum(jnp.where(mask_lane == place, masks, 0.0), axis=1, keepdims=True)
        scores = jnp.where(present[None] > 0, scores, -1e9)
        top = jnp.max(scores, axis=1, keepdims=True)
        weights = jnp.exp2(scores - top)
        weights = weights / jnp.sum(weights, axis=1, keepdims=True)
        weights = weights.astype(BF16).reshape(heads * rows, rows)
        attended.append(dot_tn(weights, spread_value))
    gated = (jnp.concatenate(attended, axis=0) * gate).astype(BF16)
    after_cols = after_rows + (dot(gated, col_out_ref[...]) + col_bias_ref[...])
    after_cols = after_cols.astype(BF16).astype(F32)

    trans_in = normalize(after_cols, ff_gain_ref[...]).astype(BF16)
    hidden = jnp.maximum(dot(trans_in, expand_ref[...]), 0.0).astype(BF16)
    updated = after_cols + dot(hidden, shrink_ref[...])
    for i in range(span):
        block = updated[i * rows : (i + 1) * rows].reshape(groups, lines, channels)
        out_ref[:, i] = block.astype(BF16)


def column_phase(mixed, table, params, heads, scale, span):
    groups, extended, lines, channels = table.shape
    residues = extended - 1
    token_block = pl.BlockSpec((groups, span, lines, channels), lambda i: (0, i, 0, 0))
    in_specs = [
        pl.BlockSpec((span, groups * lines, channels), lambda i: (i, 0, 0)),
        token_block,
        pl.BlockSpec((groups, 1, lines, channels), lambda i: (0, residues, 0, 0)),
    ]
    in_specs += [pl.BlockSpec(p.shape, lambda i: (0, 0)) for p in params]
    return pl.pallas_call(
        functools.partial(column_kernel, heads=heads, scale=scale),
        grid=(residues // span,),
        in_specs=in_specs,
        out_specs=token_block,
        out_shape=jax.ShapeDtypeStruct((groups, residues, lines, channels), BF16),
        compiler_params=pltpu.CompilerParams(vmem_limit_bytes=VMEM),
        name="column_phase",
    )(mixed, table, table, *params)


def shards(
    seq_size,
    res_size,
    homology_table,
    coupled_state,
    aligned_indicator,
    amino_indicator,
    horizontal_scaling_factor,
    horizontal_projection_matrix,
    horizontal_sigmoid_shift,
    horizontal_result_matrix,
    horizontal_result_shift,
    coupling_scaling_factor,
    coupling_head_matrix,
    downward_stretch_vector,
    vertical_projection_matrix,
    vertical_sigmoid_shift,
    vertical_result_matrix,
    vertical_result_shift,
    feedforward_scaling_factor,
    feedforward_expand_matrix,
    feedforward_shrink_matrix,
):
    lines, residues, channels = homology_table.shape
    heads = coupling_head_matrix.shape[1]
    head_size = channels // heads
    scale = LOG2E / math.sqrt(head_size)
    span = residues // seq_size
    core = lax.axis_index("res") % 2
    parity = [list(range(p, res_size, 2)) for p in (0, 1)]
    parity_all = [[r * res_size + c for r in range(seq_size) for c in group] for group in parity]

    by_residue = jnp.transpose(homology_table, (1, 0, 2)).reshape(seq_size, span, lines, channels)
    mask_row = jnp.transpose(aligned_indicator.reshape(lines, seq_size, span), (1, 0, 2))
    mask_row = jnp.pad(mask_row.astype(BF16), ((0, 0), (0, 0), (0, channels - span)))
    columns = jnp.concatenate([by_residue, mask_row[:, None]], axis=1)
    columns = lax.all_to_all(columns, "seq", 0, 0)

    tile_bias = pair_bias(coupled_state, coupling_scaling_factor, coupling_head_matrix, 32)
    rows = tile_bias.shape[1] // 2
    sent = lax.all_to_all(tile_bias.reshape(res_size, rows, residues), "res", 0, 0)
    sent = sent.reshape(res_size // 2, 2, rows, residues)
    near = lax.dynamic_index_in_dim(sent, core, 1, keepdims=True)
    far = lax.dynamic_index_in_dim(sent, 1 - core, 1, keepdims=True)
    row_bias = jnp.transpose(jnp.concatenate([near, far], axis=1), (2, 1, 0, 3))
    row_bias = row_bias.reshape(rows, res_size * residues)
    bias = lax.all_gather(row_bias, "seq", axis=0)

    present = aligned_indicator * amino_indicator[None, :]
    mask = jnp.where(present > 0, 0.0, MASKED).astype(F32)
    packed = pack_heads(
        homology_table, mask, horizontal_scaling_factor, horizontal_projection_matrix, heads, scale
    )
    own = lax.all_to_all(packed, "res", 0, 0, axis_index_groups=parity)
    other = lax.ppermute(own, "res", [(c, c ^ 1) for c in range(res_size)])

    mixed = row_attention(own, other, bias, seq_size, head_size, 2)
    mixed = mixed.reshape((seq_size * res_size // 2,) + mixed.shape[2:])
    mixed = lax.all_to_all(mixed, ("seq", "res"), 0, 0, axis_index_groups=parity_all)
    group = LANES // head_size
    mixed = mixed.reshape(seq_size, heads, lines // group, span, group, head_size)
    mixed = jnp.transpose(mixed, (3, 0, 2, 4, 1, 5)).reshape(span, seq_size * lines, channels)

    params = [
        horizontal_scaling_factor[None],
        horizontal_projection_matrix[:, 3 * channels :],
        horizontal_sigmoid_shift[None],
        horizontal_result_matrix,
        horizontal_result_shift[None],
        downward_stretch_vector[None],
        vertical_projection_matrix,
        vertical_sigmoid_shift[None],
        vertical_result_matrix,
        vertical_result_shift[None],
        feedforward_scaling_factor[None],
        feedforward_expand_matrix,
        feedforward_shrink_matrix,
    ]
    updated = column_phase(mixed, columns, params, heads, scale, 4)
    updated = lax.all_to_all(updated, "seq", 0, 0)
    return jnp.transpose(updated.reshape(residues, lines, channels), (1, 0, 2))


def solution(mesh):
    table = P("seq", "res", None)
    return jax.shard_map(
        functools.partial(shards, mesh.shape["seq"], mesh.shape["res"]),
        mesh=mesh,
        in_specs=(table, table, P("seq", "res"), P("res")) + (P(),) * 15,
        out_specs=table,
        check_vma=False,
    )
```

time: 1000 us -> 296 us (0.30)
  matrix products: 241 us -> 0 us
  blocking collectives: 245 us -> 57.7 us
  local copies, waits for them, and re-layouts: 152 us -> 20.2 us
  other arithmetic: 135 us -> 4.22 us
  waiting for transfers between devices: 209 us -> 99.4 us
  Pallas kernels: 0 us -> 83.4 us
  starting transfers between devices: 4.95 us -> 16.2 us
    all_gather x2 -> x0, blocking collectives: 245 us -> none  [the longest x1 211 us: shards(): lax.all_gather(key_present_mask, 'res', axis=1, tiled=True)]
    dot_general x25 -> x0, matrix products: 233 us -> none  [the longest x8 96.1 us: one_row(): jnp.einsum('hqk,khd->qhd', weights, vals, preferred_element_type=jnp.floa...]
    all_gather x3 -> x1, waiting for transfers between devices: 209 us -> 62.2 us  [shards(): bias = lax.all_gather(row_bias, 'seq', axis=0)]
    sub x8 -> x0, other arithmetic: 86.5 us -> none  [one_row(): weights = jax.nn.softmax(attention_logits, axis=-1).astype(jnp.bfloat16)]
    pallas_call x0 -> x4, Pallas kernels: none -> 83.4 us  [the longest x1 44.8 us: row_attention(): pl.pallas_call(functools.partial(row_kernel, per=per, head_size=head_size...]
    all_to_all x0 -> x2, blocking collectives: none -> 57.7 us  [the longest x1 39.8 us: shards(): own = lax.all_to_all(packed, 'res', 0, 0, axis_index_groups=parity)]
    convert_element_type x2, local copies, waits for them, and re-layouts: 43.9 us -> 0.09 us  [shards(): mask_row.astype(BF16)]
    all_to_all x1 -> x3, waiting for transfers between devices: 0.01 us -> 32.1 us  [the longest x1 19.2 us: shards(): lax.all_to_all(tile_bias.reshape(res_size, rows, residues), 'res', 0, 0)]
  transfers between devices with their start and end apart: 4 -> 5, of which waited for: 2 -> 4; matrix products, arithmetic and copies ran while one was open for 7% -> 5% of each run, Pallas kernels for 0% -> 2%
where the time goes in v1:
time: 296 us; the launch traced here: 295 us
  waiting for transfers between devices  99.4 us (34%)
  Pallas kernels  83.4 us (28%)
  blocking collectives  57.7 us (19%)
  local copies, waits for them, and re-layouts  20.2 us (7%)
  starting transfers between devices  16.2 us (5%)
  between operations  13.6 us (5%)
  other arithmetic  4.22 us (1%)
    all_gather x1, waiting for transfers between devices, shards(): bias = lax.all_gather(row_bias, 'seq', axis=0)  62.2 us
    pallas_call x1, Pallas kernels, row_attention(): pl.pallas_call(functools.partial(row_kernel, per=per, head_size=head_size...  44.8 us
    all_to_all x1, blocking collectives, shards(): own = lax.all_to_all(packed, 'res', 0, 0, axis_index_groups=parity)  39.8 us
    all_to_all x1, waiting for transfers between devices, shards(): lax.all_to_all(tile_bias.reshape(res_size, rows, residues), 'res', 0, 0)  19.2 us
    pallas_call x1, Pallas kernels, column_phase(): pl.pallas_call(functools.partial(column_kernel, heads=heads, scale=scale)...  18 us
    all_to_all x1, blocking collectives, shards(): updated = lax.all_to_all(updated, 'seq', 0, 0)  17.9 us
    pallas_call x1, Pallas kernels, pair_bias(): pl.pallas_call(functools.partial(pair_kernel, channels=channels, heads=he...  13.4 us
    all_to_all x1, waiting for transfers between devices, shards(): lax.all_to_all(mixed, ('seq', 'res'), 0, 0, axis_index_groups=parity_all)  12.9 us
  transfers between devices with their start and end apart: 5, of which 4 were waited for; matrix products, arithmetic and copies ran while one was open for 5% of the time, Pallas kernels for 2%

profile of v1, /device:TPU:0, one launch (start us, length us, event | category | flops | bytes accessed | tf_op | source)
XLA Modules:
  0.0 294.7 jit_solution(1279693257748407566)
XLA Ops:
  6.5 0.8 fusion.2
  7.3 0.8 bitcast_convert_fusion
  8.1 0.8 fusion
  8.9 0.6 pad_maximum_fusion.1.project_ref
  9.5 13.4 %pair_bias.1 = bf16[8,320,160]{2,1,0:T(8,128)(2,1)} custom-call(bf16[320,160,128]{2,1,0:T(8,128)(2,1)} %pair_ref.1, bf16[144,128]{1,0:T(8,128)(2,1)} %pad_maximum_fusion.1.project_ref), custom_call_target="tpu_custom_call" | custom-call | tf_op jit(solution)/shard_map/pair_bias/pallas_call | solution.py:63
  22.9 5.5 %all-to-all-start.1 = ((bf16[16,160,160]{2,1,0:T(8,128)(2,1)}), bf16[16,160,160]{2,1,0:T(8,128)(2,1)S(1)}, u32[]{:S(2)}, u32[]{:S(2)}) async-start(bf16[16,160,160]{2,1,0:T(8,128)(2,1)} %bitcast.43), calls=%async_computation.1 | async-start | bytes 2621440 | tf_op jit(solution)/shard_map/all_to_all | solution.py:300
  28.5 19.2 %all-to-all-done.1 = bf16[16,160,160]{2,1,0:T(8,128)(2,1)S(1)} async-done(((bf16[16,160,160]{2,1,0:T(8,128)(2,1)}), bf16[16,160,160]{2,1,0:T(8,128)(2,1)S(1)}, u32[]{:S(2)}, u32[]{:S(2)}) %all-to-all-start.1) | async-done | bytes 819232 | tf_op jit(solution)/shard_map/all_to_all | solution.py:300
  47.8 0.2 maximum_bitcast_fusion
  48.0 0.7 copy.44
  48.7 2.7 all_gather_reshape.3
  51.5 0.2 copy.40
  51.7 0.1 select_bitcast_fusion
  51.9 1.0 copy.43.weight_ref
  52.9 1.1 copy.42.mask_ref
  54.1 7.3 %pack_heads.1 = bf16[8,8,160,128]{3,2,1,0:T(8,128)(2,1)} custom-call(bf16[8,160,256]{2,1,0:T(8,128)(2,1)} %table_ref.1, f32[8,160,1]{2,1,0:T(8,128)} %copy.42.mask_ref, f32[1,256]{1,0:T(1,128)} %bitcast.51, bf16[256,1024]{1,0:T(8,128)(2,1)} %copy.43.weight_ref), custom_call_target="tpu_custom_call" | custom-call | tf_op jit(solution)/shard_map/pack_heads/pallas_call | solution.py:98
  61.4 39.8 %all_to_all.25.own_ref = bf16[8,8,160,128]{3,2,1,0:T(8,128)(2,1)S(1)} all-to-all(bf16[8,8,160,128]{3,2,1,0:T(8,128)(2,1)} %pack_heads.1), channel_id=1, replica_groups={{0,2,4,6,8,10,12,14},{1,3,5,7,9,11,13,15},{16,18,20,22,24,26,28,30},{17..., dimensions={0} | all-to-all | bytes 5242880 | tf_op jit(solution)/shard_map/all_to_all | solution.py:313
  101.1 5.0 %collective-permute-done.other_ref = bf16[8,8,160,128]{3,2,1,0:T(8,128)(2,1)} collective-permute-done((bf16[8,8,160,128]{3,2,1,0:T(8,128)(2,1)S(1)}, bf16[8,8,160,128]{3,2,1,0:T(8,128)(2,1)}, u32[]{:S(2)}, u32[]{:S(2)}) %collective-permute-start) | collective-permute-done | bytes 2621472 | tf_op jit(solution)/shard_map/ppermute | solution.py:314
  106.2 62.2 %all-gather.2.cloned.1.call-done.bias_ref = bf16[8,160,2560]{2,1,0:T(8,128)(2,1)} async-done(((bf16[1,160,2560]{2,1,0:T(8,128)(2,1)}), bf16[8,160,2560]{2,1,0:T(8,128)(2,1)}) %all-gather.2.cloned.1.call-update) | async-done | bytes 6553616 | tf_op jit(solution)/shard_map/all_gather | solution.py:306
  168.4 44.8 %row_attention.1 = bf16[8,8,40,128]{3,2,1,0:T(8,128)(2,1)} custom-call(bf16[8,8,160,128]{3,2,1,0:T(8,128)(2,1)} %copy-done, bf16[8,8,160,128]{3,2,1,0:T(8,128)(2,1)} %collective-permute-done.other_ref, bf16[8,160,2560]{2,1,0:T(8,128)(2,1)} %all-gather.2.cloned.1.call-done.bias_ref), custom_call_target="tpu_custom_call" | custom-call | tf_op jit(solution)/shard_map/row_attention/pallas_call | solution.py:161
  213.1 6.9 %all-to-all-start.2 = ((bf16[64,40,128]{2,1,0:T(8,128)(2,1)}), bf16[64,40,128]{2,1,0:T(8,128)(2,1)S(1)}, u32[]{:S(2)}, u32[]{:S(2)}) async-start(bf16[64,40,128]{2,1,0:T(8,128)(2,1)} %bitcast.44), calls=%async_computation.2 | async-start | bytes 1310720 | tf_op jit(solution)/shard_map/all_to_all | solution.py:318
  220.0 0.4 copy.46
  220.5 0.9 pad_maximum_fusion
  221.4 12.9 %all-to-all-done.2 = bf16[64,40,128]{2,1,0:T(8,128)(2,1)S(1)} async-done(((bf16[64,40,128]{2,1,0:T(8,128)(2,1)}), bf16[64,40,128]{2,1,0:T(8,128)(2,1)S(1)}, u32[]{:S(2)}, u32[]{:S(2)}) %all-to-all-start.2) | async-done | bytes 655392 | tf_op jit(solution)/shard_map/all_to_all | solution.py:318
  234.4 3.8 %all-to-all-start.3 = ((bf16[8,21,8,256]{3,2,1,0:T(8,128)(2,1)}), bf16[8,21,8,256]{3,2,1,0:T(8,128)(2,1)S(1)}, u32[]{:S(2)}, u32[]{:S(2)}) async-start(bf16[8,21,8,256]{3,2,1,0:T(8,128)(2,1)} %pad_maximum_fusion), calls=%async_computation.3 | async-start | bytes 1376256 | tf_op jit(solution)/shard_map/all_to_all | solution.py:296
  238.1 0.7 slice.3.row_gate_ref
  238.8 3.7 %reshape.45 = bf16[8,8,2,20,4,32]{5,4,3,2,1,0:T(4,128)(2,1)S(1)} reshape(bf16[64,40,128]{2,1,0:T(8,128)(2,1)} %copy-done.3) | data formatting | bytes 1310720 | tf_op jit(solution)/shard_map/reshape | solution.py:320
  242.5 3.2 %copy.45 = bf16[20,8,2,4,8,32]{5,4,3,2,1,0:T(8,128)(2,1)} copy(bf16[20,8,2,4,8,32]{5,3,0,2,4,1:T(4,128)(2,1)S(1)} %bitcast.41) | data formatting | bytes 1310720 | tf_op jit(solution)/shard_map/transpose | solution.py:321
  245.7 4.4 %reshape.46.mixed_ref = bf16[20,64,256]{2,1,0:T(8,128)(2,1)} reshape(bf16[20,8,2,4,8,32]{5,4,3,2,1,0:T(8,128)(2,1)} %copy.45) | data formatting | bytes 1310720 | tf_op jit(solution)/shard_map/reshape | solution.py:321
  250.1 0.9 copy-done.1
  251.0 18.0 %column_phase.1 = bf16[8,20,8,256]{3,2,1,0:T(8,128)(2,1)} custom-call(bf16[20,64,256]{2,1,0:T(8,128)(2,1)} %reshape.46.mixed_ref, bf16[8,21,8,256]{3,2,1,0:T(8,128)(2,1)} %copy-done.1, bf16[8,21,8,256]{3,2,1,0:T(8,128)(2,1)} %copy-done.1, f32[1,256]{1,0:T(1,128)} %bitcast.52, bf16[256,256]{1,0:T(8,128)(2,1)} %slice.3.row_gate_ref, f32[1,256]{1,0:T(1,128)} %bitcast.53, ...), custom_call_target="tpu_custom_call" | custom-call | tf_op jit(solution)/shard_map/column_phase/pallas_call | solution.py:249
  269.0 17.9 %all_to_all.26 = bf16[8,20,8,256]{3,2,1,0:T(8,128)(2,1)S(1)} all-to-all(bf16[8,20,8,256]{3,2,1,0:T(8,128)(2,1)} %column_phase.1), channel_id=1, replica_groups=mesh['seq'=8,'res'=16] {'seq'}, dimensions={0} | all-to-all | bytes 1310720 | tf_op jit(solution)/shard_map/all_to_all | solution.py:339
  286.9 1.0 copy.51
  (27 shorter events, 0.4 us)
Async XLA Ops:
  22.9 24.8 %all-to-all-start.1 = ((bf16[16,160,160]{2,1,0:T(8,128)(2,1)}), bf16[16,160,160]{2,1,0:T(8,128)(2,1)S(1)}, u32[]{:S(2)}, u32[]{:S(2)}) async-start(bf16[16,160,160]{2,1,0:T(8,128)(2,1)} %bitcast.43), calls=%async_computation.1 | async-start | bytes 2621440 | tf_op jit(solution)/shard_map/all_to_all | solution.py:300
  28.4 140.0 %all-gather.2.cloned.1.call-start = ((), (), s32[]{:S(2)}) async-start(), calls=%async_computation.5 | async-start | bytes 7372800 | tf_op jit(solution)/shard_map/all_gather | solution.py:306
  48.7 2.8 copy-start.4
  51.9 1.1 copy-start.5
  51.9 1.1 copy-start.6
  101.1 67.2 %copy-start = (bf16[8,8,160,128]{3,2,1,0:T(8,128)(2,1)}, bf16[8,8,160,128]{3,2,1,0:T(8,128)(2,1)S(1)}, u32[]{:S(2)}) copy-start(bf16[8,8,160,128]{3,2,1,0:T(8,128)(2,1)S(1)} %all_to_all.25.own_ref) | copy-start | bytes 7864324
  101.1 5.0 %collective-permute-start = (bf16[8,8,160,128]{3,2,1,0:T(8,128)(2,1)S(1)}, bf16[8,8,160,128]{3,2,1,0:T(8,128)(2,1)}, u32[]{:S(2)}, u32[]{:S(2)}) collective-permute-start(bf16[8,8,160,128]{3,2,1,0:T(8,128)(2,1)S(1)} %all_to_all.25.own_ref), channel_id=1, source_target_pairs={{0,1},{1,0},{2,3},{3,2},{4,5},{5,4},{6,7},{7,6},{8,9},{9,8},{10,11... | collective-permute-start | bytes 7864328 | tf_op jit(solution)/shard_map/ppermute | solution.py:314
  213.1 6.9 %copy-start.2 = (bf16[8,160,256]{2,1,0:T(8,128)(2,1)S(1)}, bf16[8,160,256]{2,1,0:T(8,128)(2,1)}, u32[]{:S(2)}) copy-start(bf16[8,160,256]{2,1,0:T(8,128)(2,1)} %table_ref.1) | copy-start | bytes 1966084
  213.1 21.2 %all-to-all-start.2 = ((bf16[64,40,128]{2,1,0:T(8,128)(2,1)}), bf16[64,40,128]{2,1,0:T(8,128)(2,1)S(1)}, u32[]{:S(2)}, u32[]{:S(2)}) async-start(bf16[64,40,128]{2,1,0:T(8,128)(2,1)} %bitcast.44), calls=%async_computation.2 | async-start | bytes 1310720 | tf_op jit(solution)/shard_map/all_to_all | solution.py:318
  234.4 3.8 %copy-start.3 = (bf16[64,40,128]{2,1,0:T(8,128)(2,1)}, bf16[64,40,128]{2,1,0:T(8,128)(2,1)S(1)}, u32[]{:S(2)}) copy-start(bf16[64,40,128]{2,1,0:T(8,128)(2,1)S(1)} %all-to-all-done.2) | copy-start | bytes 1966084
  234.4 15.8 %all-to-all-start.3 = ((bf16[8,21,8,256]{3,2,1,0:T(8,128)(2,1)}), bf16[8,21,8,256]{3,2,1,0:T(8,128)(2,1)S(1)}, u32[]{:S(2)}, u32[]{:S(2)}) async-start(bf16[8,21,8,256]{3,2,1,0:T(8,128)(2,1)} %pad_maximum_fusion), calls=%async_computation.3 | async-start | bytes 1376256 | tf_op jit(solution)/shard_map/all_to_all | solution.py:296
  250.1 0.9 copy-start.1
Sparse Core Ops, SparseCore 0:
  51.6 116.6 all-gather.1
